TPU v7x, 256 devices: a whole 4x4x8 slice. The times are simulated.
256 devices in a mesh: dp: 2 (over core), frame: 16 (over x, y), mp: 8 (over z).
Axes of the slice: x: 4, y: 4, z: 8, core: 2. Of those that a mesh axis runs over, the one named last changes fastest.
Arguments:
- frames_in: bfloat16 [2, 16, 1024, 768], P('dp', 'frame'), may hold values from -6 to 6
- gain_space: float32 [768], replicated, may hold values from 0.1 to 1.9
- space_proj: bfloat16 [3, 768, 512], P(None, None, 'mp'), may hold values from -0.21875 to 0.21875
- space_out: bfloat16 [512, 768], replicated, may hold values from -0.25 to 0.25
- gain_time: float32 [768], replicated, may hold values from 0.1 to 1.9
- time_proj: bfloat16 [3, 768, 768], replicated, may hold values from -0.21875 to 0.21875
- time_out: bfloat16 [768, 768], replicated, may hold values from -0.21875 to 0.21875
- gain_mlp: float32 [768], replicated, may hold values from 0.1 to 1.9
- mlp_in: bfloat16 [3072, 768], P(('frame', 'mp')), may hold values from -0.21875 to 0.21875
- mlp_out: bfloat16 [3072, 768], P(('frame', 'mp')), may hold values from -0.109375 to 0.109375
- code_proj: bfloat16 [768, 32], replicated, may hold values from -0.21875 to 0.21875
- code_index: int32 [2, 16, 1024], P('dp', None, ('frame', 'mp')), may hold values from 0 to 1023, as said below
Outputs:
- block_out: bfloat16 [2, 16, 1024, 768], P('dp', None, ('frame', 'mp'))
- code_means: float32 [1024, 32], replicated
Inputs may be any that keep to these rules, and one draw needn't show every extreme that they name: `code_index`: at least 128 codes are named by no token; which ones is drawn from the seed.
All inputs are finite; a program needn't handle non-finite values.
Results may differ from a plain program's by a relative error of at most 0.017.
Values may be sent and summed in bfloat16 or wider, within the bound.
A program may use at most 64 MiB of HBM per device.

v0:
```python
import math
import jax
import jax.numpy as jnp
from jax import lax
from jax.sharding import PartitionSpec as P

HD = 64
CODES = 1024


def layer_norm(values, gain):
    center = jnp.mean(values, axis=-1, keepdims=True)
    spread = jnp.mean((values - center) ** 2, axis=-1, keepdims=True)
    return (values - center) * lax.rsqrt(spread + 1e-06) * gain


def attend_frame(queries, keys, values, factor):
    positions, heads_n, head_size = queries.shape
    block_rows = math.gcd(positions, 512)
    query_blocks = queries.reshape(positions // block_rows, block_rows, heads_n, head_size)

    def per_block(query_block):
        scores = (
            jnp.einsum("qhd,khd->hqk", query_block, keys, preferred_element_type=jnp.float32)
            * factor
        )
        weights = jax.nn.softmax(scores, axis=-1).astype(jnp.bfloat16)
        return jnp.einsum(
            "hqk,khd->qhd", weights, values, preferred_element_type=jnp.float32
        ).astype(jnp.bfloat16)

    return lax.map(per_block, query_blocks).reshape(positions, heads_n * head_size)


def attend_time(queries, keys, values, factor):
    frames_n = queries.shape[0]
    scores = (
        jnp.einsum("fnhd,gnhd->nhfg", queries, keys, preferred_element_type=jnp.float32) * factor
    )
    later = lax.broadcasted_iota(jnp.int32, (frames_n, frames_n), 0)
    earlier = lax.broadcasted_iota(jnp.int32, (frames_n, frames_n), 1)
    scores = jnp.where(earlier <= later, scores, -jnp.inf)
    weights = jax.nn.softmax(scores, axis=-1).astype(jnp.bfloat16)
    return jnp.einsum(
        "nhfg,gnhd->fnhd", weights, values, preferred_element_type=jnp.float32
    ).astype(jnp.bfloat16)


def unit_block(tokens, rows_in, rows_out):
    pre_act = lax.dot_general(
        tokens, rows_in, (((1,), (1,)), ((), ())), preferred_element_type=jnp.float32
    )
    hidden = jax.nn.gelu(pre_act, approximate=True).astype(jnp.bfloat16)
    return jnp.dot(hidden, rows_out, preferred_element_type=jnp.float32)


def shards(
    frames_in,
    gain_space,
    space_proj,
    space_out,
    gain_time,
    time_proj,
    time_out,
    gain_mlp,
    mlp_in,
    mlp_out,
    code_proj,
    code_index,
):
    factor = 1.0 / math.sqrt(HD)
    tokens = frames_in[0, 0]
    positions, features = tokens.shape
    normed = layer_norm(tokens.astype(jnp.float32), gain_space).astype(jnp.bfloat16)
    projected = jnp.einsum(
        "pd,sdc->spc", normed, space_proj, preferred_element_type=jnp.float32
    ).astype(jnp.bfloat16)
    heads_here = space_proj.shape[2] // HD
    projected = projected.reshape(3, positions, heads_here, HD)
    local_heads = attend_frame(projected[0], projected[1], projected[2], factor)
    col_width = features // lax.axis_size("mp")
    own_cols = lax.dynamic_slice_in_dim(tokens, lax.axis_index("mp") * col_width, col_width, 1)
    heads_all, token_rows = (
        lax.all_to_all(
            lax.all_to_all(local_heads[None], "frame", split_axis=1, concat_axis=0, tiled=True),
            "mp",
            split_axis=1,
            concat_axis=2,
            tiled=True,
        ),
        lax.all_to_all(
            lax.all_to_all(own_cols[None], "frame", split_axis=1, concat_axis=0, tiled=True),
            "mp",
            split_axis=1,
            concat_axis=2,
            tiled=True,
        ),
    )
    frames_n, pos_n, _ = token_rows.shape
    row_count = frames_n * pos_n
    after_space = token_rows.reshape(row_count, features).astype(jnp.float32) + jnp.dot(
        heads_all.reshape(row_count, -1), space_out, preferred_element_type=jnp.float32
    )
    time_in = layer_norm(after_space, gain_time).astype(jnp.bfloat16)
    time_qkv = jnp.einsum(
        "rd,sdc->src", time_in, time_proj, preferred_element_type=jnp.float32
    ).astype(jnp.bfloat16)
    time_qkv = time_qkv.reshape(3, frames_n, pos_n, features // HD, HD)
    time_heads = attend_time(time_qkv[0], time_qkv[1], time_qkv[2], factor).reshape(
        row_count, features
    )
    after_time = after_space + jnp.dot(time_heads, time_out, preferred_element_type=jnp.float32)
    mlp_act = layer_norm(after_time, gain_mlp).astype(jnp.bfloat16)
    after_mlp = after_time + unit_block(
        mlp_act,
        lax.all_gather(mlp_in, ("frame", "mp"), axis=0, tiled=True),
        lax.all_gather(mlp_out, ("frame", "mp"), axis=0, tiled=True),
    )
    outputs = after_mlp.astype(jnp.bfloat16)
    code_vec = jnp.dot(outputs, code_proj, preferred_element_type=jnp.float32)
    own_codes = code_index.reshape(row_count)
    onehot = (own_codes[:, None] == lax.broadcasted_iota(jnp.int32, (1, CODES), 1)).astype(
        jnp.float32
    )
    code_sums = lax.dot_general(
        onehot,
        code_vec,
        (((0,), (0,)), ((), ())),
        precision=lax.Precision.HIGHEST,
        preferred_element_type=jnp.float32,
    )
    code_counts = jnp.sum(onehot, axis=0)
    code_sums, code_counts = lax.psum((code_sums, code_counts), ("dp", "frame", "mp"))
    code_means = code_sums / jnp.maximum(code_counts, 1.0)[:, None]
    return (outputs.reshape(1, frames_n, pos_n, features), code_means)


def solution(mesh):
    placed = (
        P("dp", "frame", None, None),
        P(),
        P(None, None, "mp"),
        P(),
        P(),
        P(),
        P(),
        P(),
        P(("frame", "mp"), None),
        P(("frame", "mp"), None),
        P(),
        P("dp", None, ("frame", "mp")),
    )
    return jax.shard_map(
        shards,
        mesh=mesh,
        in_specs=placed,
        out_specs=(P("dp", None, ("frame", "mp"), None), P()),
        check_vma=False,
    )
```

profile of v0, /device:TPU:8, one launch (start us, length us, event | category | flops | bytes accessed | tf_op | source)
XLA Modules:
  0.0 506.3 jit_solution(569047426339073134)
XLA Ops:
  8.7 1.8 convert_reduce_fusion
  12.9 1.6 reshape_squeeze.3
  14.6 1.6 copy.80
  16.1 6.7 %while.10 = (s32[]{:T(128)}, bf16[2,512,1,64]{1,3,2,0:T(8,128)(2,1)}, bf16[2,512,1,64]{1,3,2,0:T(8,128)(2,1)}, bf16[1024,1,64]{0,2,1:T(8,128)(2,1)}, bf16[1024,1,64]{0,2,1:T(8,128)(2,1)}, /*index=5*/s32[]{:T(128)}) while((s32[]{:T(128)}, bf16[2,512,1,64]{1,3,2,0:T(8,128)(2,1)}, bf16[2,512,1,64]{1,3,2,0:T(8,128)(2,1)}, ...), condition=%wide.region_5.6_spmd, body=%wide.region_2.5_spmd.sunk | while | flops 138968064 | bytes 7220321 | solution.py:32
  16.1 1.5 multiply_reduce_fusion.4
  18.2 1.3 fusion.87
  19.5 1.5 multiply_reduce_fusion.4
  21.5 1.3 fusion.87
  22.8 1.7 copy.94
  24.6 2.6 reshape.124
  27.8 3.8 reduce.6
  31.7 1.8 reshape.128
  33.5 7.4 %all-to-all-start.2 = ((bf16[16,2,2048]{2,1,0:T(2,128)(2,1)}), bf16[16,2,2048]{2,1,0:T(2,128)(2,1)}, u32[]{:S(2)}, u32[]{:S(2)}) async-start(bf16[16,2,2048]{2,1,0:T(2,128)(2,1)} %reshape.128), calls=%async_computation.2 | async-start | bytes 262144 | tf_op jit(solution)/shard_map/all_to_all | solution.py:85
  40.9 1.9 constant_dynamic-slice_fusion
  42.8 1.8 copy.101
  44.5 1.9 copy.76
  46.5 3.8 reduce.5
  50.3 2.1 reshape.126
  52.4 7.2 %all-to-all-start = ((bf16[16,2,3072]{2,1,0:T(2,128)(2,1)}), bf16[16,2,3072]{2,1,0:T(2,128)(2,1)}, u32[]{:S(2)}, u32[]{:S(2)}) async-start(bf16[16,2,3072]{2,1,0:T(2,128)(2,1)} %reshape.126), calls=%async_computation | async-start | bytes 393216 | tf_op jit(solution)/shard_map/all_to_all | solution.py:92
  59.6 1.9 reshape.129
  61.5 1.1 copy.100
  63.4 1.9 reshape.130
  65.3 1.1 all-to-all-done
  66.4 8.4 %all-to-all-start.3 = ((bf16[8,2,4096]{2,1,0:T(2,128)(2,1)}), bf16[8,2,4096]{2,1,0:T(2,128)(2,1)}, u32[]{:S(2)}, u32[]{:S(2)}) async-start(bf16[8,2,4096]{2,1,0:T(2,128)(2,1)} %reshape.130), calls=%async_computation.3 | async-start | bytes 262144 | tf_op jit(solution)/shard_map/all_to_all | solution.py:84
  74.8 2.0 reshape.127
  76.8 1.1 copy.99
  78.8 5.9 %all-to-all-done.3 = bf16[8,2,4096]{2,1,0:T(2,128)(2,1)} async-done(((bf16[8,2,4096]{2,1,0:T(2,128)(2,1)}), bf16[8,2,4096]{2,1,0:T(2,128)(2,1)}, u32[]{:S(2)}, u32[]{:S(2)}) %all-to-all-start.3) | async-done | bytes 131104 | tf_op jit(solution)/shard_map/all_to_all | solution.py:84
  84.6 4.0 all-to-all-start.1
  89.0 75.9 %psum.15 = f32[1024]{0:T(1024)S(1)} all-reduce(f32[1024]{0:T(1024)S(1)} %convert_reduce_fusion.1), channel_id=1, replica_groups=mesh['dp'=2,'frame'=16,'mp'=8] {'dp','frame','mp'}, use_global_device_ids=true, to_apply=%region_14.15 | all-reduce | flops 1024 | bytes 8192 | tf_op jit(solution)/shard_map/psum | solution.py:133
  165.0 1.8 reshape.131
  166.8 1.8 copy.86
  168.6 1.8 reshape.116
  172.3 2.0 reshape.119
  174.3 1.6 fusion.65
  177.7 2.1 squeeze.21
  179.8 2.1 squeeze.22
  181.9 2.1 squeeze.20
  183.9 1.8 fusion.32
  187.5 2.9 fusion.34
  190.4 1.9 copy.91
  192.4 2.1 reshape.117
  194.4 1.8 fusion.67
  197.7 52.6 %all-gather.5.cloned.1.call-done = bf16[3072,768]{1,0:T(8,128)(2,1)} async-done(((bf16[24,768]{1,0:T(8,128)(2,1)}), bf16[3072,768]{1,0:T(8,128)(2,1)}) %all-gather.5.cloned.1.call-update) | async-done | bytes 4718608 | tf_op jit(solution)/shard_map/all_gather | solution.py:117
  250.4 7.0 %fusion.35 = bf16[128,768]{1,0:T(8,128)(2,1)} fusion(f32[128,768]{1,0:T(8,128)} %copy-done.3, bf16[3072,768]{1,0:T(8,128)(2,1)} %all-gather.5.cloned.1.call-done, bf16[3072,768]{1,0:T(8,128)(2,1)} %all-gather.3.cloned.1.call-done, f32[768]{0:T(1024)S(1)} %copy-done.9, f32[128]{0:T(128)} %add_rsqrt_fusion.1, f32[128]{0:T(128)S(1)} %broadcast_multiply_fusion.1), kind=kOutput, calls=%fused_computation.47 | convolution fusion | flops 1212088320 | bytes 10031104 | tf_op jit(solution)/shard_map/dot_general | solution.py:54
  257.3 1.1 fusion.68
  258.4 1.1 fusion.41
  259.5 238.7 %all-reduce.2.cloned.1.call-done = f32[1024,32]{0,1:T(8,128)} async-done(((f32[1024,32]{0,1:T(8,128)}), f32[1024,32]{0,1:T(8,128)}) %all-reduce.2.cloned.1.call-update) | async-done | bytes 131088 | tf_op jit(solution)/shard_map/psum | solution.py:133
  498.2 1.6 broadcast_divide_fusion
  (61 shorter events, 14.5 us)
Async XLA Ops:
  7.2 169.0 %copy-start = (bf16[3,768,768]{2,1,0:T(8,128)(2,1)S(1)}, bf16[3,768,768]{2,1,0:T(8,128)(2,1)}, u32[]{:S(2)}) copy-start(bf16[3,768,768]{2,1,0:T(8,128)(2,1)} %param.19) | copy-start | bytes 10616836
  7.2 4.0 copy-start.8
  7.2 190.6 %all-gather.3.cloned.1.call-start = ((), (), s32[]{:S(2)}) async-start(), calls=%async_computation.4 | async-start | bytes 4755456 | tf_op jit(solution)/shard_map/all_gather | solution.py:116
  7.9 242.4 %all-gather.5.cloned.1.call-start = ((), (), s32[]{:S(2)}) async-start(), calls=%async_computation.5 | async-start | bytes 4755456 | tf_op jit(solution)/shard_map/all_gather | solution.py:117
  8.7 1.9 copy-start.1
  8.7 2.5 copy-start.7
  16.1 2.0 copy-start.4
  19.5 2.0 copy-start.4
  33.5 18.9 %all-to-all-start.2 = ((bf16[16,2,2048]{2,1,0:T(2,128)(2,1)}), bf16[16,2,2048]{2,1,0:T(2,128)(2,1)}, u32[]{:S(2)}, u32[]{:S(2)}) async-start(bf16[16,2,2048]{2,1,0:T(2,128)(2,1)} %reshape.128), calls=%async_computation.2 | async-start | bytes 262144 | tf_op jit(solution)/shard_map/all_to_all | solution.py:85
  52.4 14.0 %all-to-all-start = ((bf16[16,2,3072]{2,1,0:T(2,128)(2,1)}), bf16[16,2,3072]{2,1,0:T(2,128)(2,1)}, u32[]{:S(2)}, u32[]{:S(2)}) async-start(bf16[16,2,3072]{2,1,0:T(2,128)(2,1)} %reshape.126), calls=%async_computation | async-start | bytes 393216 | tf_op jit(solution)/shard_map/all_to_all | solution.py:92
  61.5 27.3 %copy-start.5 = (s32[1,16,8]{1,2,0:T(8,128)S(1)}, s32[1,16,8]{1,2,0:T(8,128)}, u32[]{:S(2)}) copy-start(s32[1,16,8]{1,2,0:T(8,128)} %param.25) | copy-start | bytes 1540
  66.4 18.3 %all-to-all-start.3 = ((bf16[8,2,4096]{2,1,0:T(2,128)(2,1)}), bf16[8,2,4096]{2,1,0:T(2,128)(2,1)}, u32[]{:S(2)}, u32[]{:S(2)}) async-start(bf16[8,2,4096]{2,1,0:T(2,128)(2,1)} %reshape.130), calls=%async_computation.3 | async-start | bytes 262144 | tf_op jit(solution)/shard_map/all_to_all | solution.py:84
  84.6 85.8 %all-to-all-start.1 = ((bf16[16,64,96]{2,0,1:T(8,128)(2,1)}), bf16[16,64,96]{2,0,1:T(8,128)(2,1)}, u32[]{:S(2)}, u32[]{:S(2)}) async-start(bf16[16,64,96]{2,0,1:T(8,128)(2,1)} %copy.77), calls=%async_computation.1 | async-start | bytes 524288 | tf_op jit(solution)/shard_map/all_to_all | solution.py:91
  88.7 409.5 %all-reduce.2.cloned.1.call-start = ((), (), s32[]{:S(2)}) async-start(), calls=%async_computation.6 | async-start | bytes 262144 | tf_op jit(solution)/shard_map/psum | solution.py:133
  171.4 4.7 copy-start.6
  176.0 0.9 copy-start.2
  185.7 0.9 copy-start.10
  190.4 59.9 %copy-start.9 = (f32[768]{0:T(1024)S(1)}, f32[768]{0:T(1024)}, u32[]{:S(2)}) copy-start(f32[768]{0:T(1024)} %param.21) | copy-start | bytes 9220
  196.3 0.7 copy-start.3
Sparse Core Ops, SparseCore 0:
  11.7 120.9 all-gather.2
  136.3 113.9 all-gather.4
  259.6 238.5 all-reduce.1
where the time goes:
time: 508 us; the launch traced here: 506 us
  waiting for transfers between devices  300 us (59%)
  blocking collectives  75.9 us (15%)
  local copies, waits for them, and re-layouts  49.2 us (10%)
  starting transfers between devices  27.2 us (5%)
  matrix products  24.5 us (5%)
  other arithmetic  15.8 us (3%)
  between operations  14 us (3%)
    psum x1, waiting for transfers between devices, shards(): lax.psum((code_sums, code_counts), ('dp', 'frame', 'mp'))  239 us
    psum x1, blocking collectives, shards(): lax.psum((code_sums, code_counts), ('dp', 'frame', 'mp'))  75.9 us
    all_gather x1, waiting for transfers between devices, shards(): lax.all_gather(mlp_out, ('frame', 'mp'), axis=0, tiled=True)  52.6 us
    unnamed x31, local copies, waits for them, and re-layouts  17.7 us
  transfers between devices with their start and end apart: 7, of which 4 were waited for; matrix products, arithmetic and copies ran while one was open for 15% of the time, Pallas kernels for 0%

commit v1 on v0

--- a/solution.py
+++ b/solution.py
@@ -114,7 +114,12 @@
     after_mlp = after_time + unit_block(
         mlp_act,
         lax.all_gather(mlp_in, ("frame", "mp"), axis=0, tiled=True),
-        lax.all_gather(mlp_out, ("frame", "mp"), axis=0, tiled=True),
+        jnp.concatenate(
+            lax.all_to_all(
+                jnp.stack([mlp_out] * lax.axis_size(("frame", "mp"))), ("frame", "mp"), 0, 0
+            ),
+            axis=0,
+        ),
     )
     outputs = after_mlp.astype(jnp.bfloat16)
     code_vec = jnp.dot(outputs, code_proj, preferred_element_type=jnp.float32)

time: 508 us -> 549 us (1.081)
  blocking collectives: 75.9 us -> 163 us
  waiting for transfers between devices: 300 us -> 246 us
    psum x1, blocking collectives: 75.9 us -> 149 us  [shards(): lax.psum((code_sums, code_counts), ('dp', 'frame', 'mp'))]
    all_gather x1 -> x0, waiting for transfers between devices: 52.6 us -> none  [shards(): lax.all_gather(mlp_out, ('frame', 'mp'), axis=0, tiled=True)]
    all_to_all x0 -> x1, blocking collectives: none -> 14.5 us  [shards(): lax.all_to_all(lax.all_to_all(own_cols[None], 'frame', split_axis=1, conc...]
  transfers between devices with their start and end apart: 7 -> 6, of which waited for: 4 -> 3; matrix products, arithmetic and copies ran while one was open for 15% -> 10% of each run, Pallas kernels for 0% -> 0%
where the time goes in v1:
time: 549 us; the launch traced here: 547 us
  waiting for transfers between devices  246 us (45%)
  blocking collectives  163 us (30%)
  local copies, waits for them, and re-layouts  52.6 us (10%)
  starting transfers between devices  31.4 us (6%)
  matrix products  24.4 us (4%)
  other arithmetic  15.6 us (3%)
  between operations  14.3 us (3%)
    psum x1, waiting for transfers between devices, shards(): lax.psum((code_sums, code_counts), ('dp', 'frame', 'mp'))  239 us
    psum x1, blocking collectives, shards(): lax.psum((code_sums, code_counts), ('dp', 'frame', 'mp'))  149 us
    unnamed x31, local copies, waits for them, and re-layouts  17.7 us
    all_to_all x1, blocking collectives, shards(): lax.all_to_all(lax.all_to_all(own_cols[None], 'frame', split_axis=1, conc...  14.5 us
  transfers between devices with their start and end apart: 6, of which 3 were waited for; matrix products, arithmetic and copies ran while one was open for 10% of the time, Pallas kernels for 0%

profile of v1, /device:TPU:8, one launch (start us, length us, event | category | flops | bytes accessed | tf_op | source)
XLA Modules:
  0.0 547.4 jit_solution(5408309880271126670)
XLA Ops:
  7.2 1.8 convert_reduce_fusion
  11.6 1.6 reshape_squeeze.3
  13.2 1.6 copy.80
  14.8 6.7 %while.10 = (s32[]{:T(128)}, bf16[2,512,1,64]{1,3,2,0:T(8,128)(2,1)}, bf16[2,512,1,64]{1,3,2,0:T(8,128)(2,1)}, bf16[1024,1,64]{0,2,1:T(8,128)(2,1)}, bf16[1024,1,64]{0,2,1:T(8,128)(2,1)}, /*index=5*/s32[]{:T(128)}) while((s32[]{:T(128)}, bf16[2,512,1,64]{1,3,2,0:T(8,128)(2,1)}, bf16[2,512,1,64]{1,3,2,0:T(8,128)(2,1)}, ...), condition=%wide.region_5.6_spmd, body=%wide.region_2.5_spmd.sunk | while | flops 138968064 | bytes 7220321 | solution.py:32
  14.8 1.5 multiply_reduce_fusion.4
  16.9 1.3 fusion.87
  18.2 1.5 multiply_reduce_fusion.4
  20.2 1.3 fusion.87
  21.5 1.7 copy.94
  23.3 2.6 reshape.130
  26.4 3.7 reduce.6
  30.1 1.8 reshape.134
  32.0 7.4 %all-to-all-start.2 = ((bf16[16,2,2048]{2,1,0:T(2,128)(2,1)}), bf16[16,2,2048]{2,1,0:T(2,128)(2,1)}, u32[]{:S(2)}, u32[]{:S(2)}) async-start(bf16[16,2,2048]{2,1,0:T(2,128)(2,1)} %reshape.134), calls=%async_computation.2 | async-start | bytes 262144 | tf_op jit(solution)/shard_map/all_to_all | solution.py:85
  39.4 1.9 constant_dynamic-slice_fusion
  41.3 1.8 copy.101
  43.0 2.0 copy.76
  45.0 3.7 reduce.5
  48.7 2.1 reshape.132
  50.8 7.2 %all-to-all-start = ((bf16[16,2,3072]{2,1,0:T(2,128)(2,1)}), bf16[16,2,3072]{2,1,0:T(2,128)(2,1)}, u32[]{:S(2)}, u32[]{:S(2)}) async-start(bf16[16,2,3072]{2,1,0:T(2,128)(2,1)} %reshape.132), calls=%async_computation | async-start | bytes 393216 | tf_op jit(solution)/shard_map/all_to_all | solution.py:92
  58.0 1.8 reshape.135
  59.8 1.1 copy.100
  61.8 1.9 reshape.136
  63.6 1.1 all-to-all-done
  64.8 8.5 %all-to-all-start.3 = ((bf16[8,2,4096]{2,1,0:T(2,128)(2,1)}), bf16[8,2,4096]{2,1,0:T(2,128)(2,1)}, u32[]{:S(2)}, u32[]{:S(2)}) async-start(bf16[8,2,4096]{2,1,0:T(2,128)(2,1)} %reshape.136), calls=%async_computation.3 | async-start | bytes 262144 | tf_op jit(solution)/shard_map/all_to_all | solution.py:84
  73.2 2.0 reshape.133
  75.2 1.1 copy.99
  77.1 5.3 all-to-all-done.3
  82.4 14.5 %all_to_all.53 = bf16[16,64,96]{2,0,1:T(8,128)(2,1)} all-to-all(bf16[16,64,96]{2,0,1:T(8,128)(2,1)} %copy.77), channel_id=1, replica_groups=mesh['dp'=2,'frame'=16,'mp'=8] {'mp'}, dimensions={1} | all-to-all | bytes 393216 | tf_op jit(solution)/shard_map/all_to_all | solution.py:91
  96.9 3.3 stack.2
  100.2 8.0 %all-to-all-start.4 = ((bf16[128,24,768]{2,1,0:T(8,128)(2,1)}), bf16[128,24,768]{2,1,0:T(8,128)(2,1)}, u32[]{:S(2)}, u32[]{:S(2)}) async-start(bf16[128,24,768]{2,1,0:T(8,128)(2,1)} %stack.2), calls=%async_computation.4 | async-start | bytes 9437184 | tf_op jit(solution)/shard_map/all_to_all | solution.py:118
  109.5 148.6 %psum.15 = f32[1024]{0:T(1024)S(1)} all-reduce(f32[1024]{0:T(1024)S(1)} %convert_reduce_fusion.1), channel_id=1, replica_groups=mesh['dp'=2,'frame'=16,'mp'=8] {'dp','frame','mp'}, use_global_device_ids=true, to_apply=%region_14.15 | all-reduce | flops 1024 | bytes 8192 | tf_op jit(solution)/shard_map/psum | solution.py:138
  258.2 1.8 reshape.137
  259.9 1.8 copy.86
  261.8 1.8 reshape.121
  265.5 2.0 reshape.125
  267.5 1.6 fusion.65
  270.9 2.1 squeeze.21
  273.0 2.1 squeeze.22
  275.1 2.1 squeeze.20
  277.1 1.8 fusion.32
  280.8 2.8 fusion.34
  283.6 2.0 copy.91
  285.6 2.1 reshape.122
  287.6 1.8 fusion.67
  290.9 7.0 %fusion.35 = bf16[128,768]{1,0:T(8,128)(2,1)} fusion(f32[128,768]{1,0:T(8,128)} %copy-done.3, bf16[3072,768]{1,0:T(8,128)(2,1)} %bitcast.23, bf16[3072,768]{1,0:T(8,128)(2,1)} %all-gather.2.cloned.1.call-done, f32[768]{0:T(1024)S(1)} %copy-done.9, f32[128]{0:T(128)} %add_rsqrt_fusion.1, f32[128]{0:T(128)S(1)} %broadcast_multiply_fusion.1), kind=kOutput, calls=%fused_computation.47 | convolution fusion | flops 1212088320 | bytes 10031104 | tf_op jit(solution)/shard_map/dot_general | solution.py:54
  299.0 1.1 fusion.41
  300.1 238.9 %all-reduce.2.cloned.1.call-done = f32[1024,32]{0,1:T(8,128)} async-done(((f32[1024,32]{0,1:T(8,128)}), f32[1024,32]{0,1:T(8,128)}) %all-reduce.2.cloned.1.call-update) | async-done | bytes 131088 | tf_op jit(solution)/shard_map/psum | solution.py:138
  539.0 1.6 broadcast_divide_fusion
  (60 shorter events, 15.0 us)
Async XLA Ops:
  7.2 262.2 %copy-start = (bf16[3,768,768]{2,1,0:T(8,128)(2,1)S(1)}, bf16[3,768,768]{2,1,0:T(8,128)(2,1)}, u32[]{:S(2)}) copy-start(bf16[3,768,768]{2,1,0:T(8,128)(2,1)} %param.19) | copy-start | bytes 10616836
  7.2 2.7 copy-start.8
  7.2 2.0 copy-start.1
  7.2 2.7 copy-start.7
  14.8 2.0 copy-start.4
  18.2 2.0 copy-start.4
  32.0 18.8 %all-to-all-start.2 = ((bf16[16,2,2048]{2,1,0:T(2,128)(2,1)}), bf16[16,2,2048]{2,1,0:T(2,128)(2,1)}, u32[]{:S(2)}, u32[]{:S(2)}) async-start(bf16[16,2,2048]{2,1,0:T(2,128)(2,1)} %reshape.134), calls=%async_computation.2 | async-start | bytes 262144 | tf_op jit(solution)/shard_map/all_to_all | solution.py:85
  50.8 14.0 %all-to-all-start = ((bf16[16,2,3072]{2,1,0:T(2,128)(2,1)}), bf16[16,2,3072]{2,1,0:T(2,128)(2,1)}, u32[]{:S(2)}, u32[]{:S(2)}) async-start(bf16[16,2,3072]{2,1,0:T(2,128)(2,1)} %reshape.132), calls=%async_computation | async-start | bytes 393216 | tf_op jit(solution)/shard_map/all_to_all | solution.py:92
  64.8 17.7 %all-to-all-start.3 = ((bf16[8,2,4096]{2,1,0:T(2,128)(2,1)}), bf16[8,2,4096]{2,1,0:T(2,128)(2,1)}, u32[]{:S(2)}, u32[]{:S(2)}) async-start(bf16[8,2,4096]{2,1,0:T(2,128)(2,1)} %reshape.136), calls=%async_computation.3 | async-start | bytes 262144 | tf_op jit(solution)/shard_map/all_to_all | solution.py:84
  100.2 9.0 %copy-start.5 = (s32[1,16,8]{1,2,0:T(8,128)S(1)}, s32[1,16,8]{1,2,0:T(8,128)}, u32[]{:S(2)}) copy-start(s32[1,16,8]{1,2,0:T(8,128)} %param.25) | copy-start | bytes 1540
  100.2 190.7 %all-to-all-start.4 = ((bf16[128,24,768]{2,1,0:T(8,128)(2,1)}), bf16[128,24,768]{2,1,0:T(8,128)(2,1)}, u32[]{:S(2)}, u32[]{:S(2)}) async-start(bf16[128,24,768]{2,1,0:T(8,128)(2,1)} %stack.2), calls=%async_computation.4 | async-start | bytes 9437184 | tf_op jit(solution)/shard_map/all_to_all | solution.py:118
  108.2 182.7 %all-gather.2.cloned.1.call-start = ((), (), s32[]{:S(2)}) async-start(), calls=%async_computation.5 | async-start | bytes 4755456 | tf_op jit(solution)/shard_map/all_gather | solution.py:116
  109.0 430.0 %all-reduce.2.cloned.1.call-start = ((), (), s32[]{:S(2)}) async-start(), calls=%async_computation.6 | async-start | bytes 262144 | tf_op jit(solution)/shard_map/psum | solution.py:138
  264.6 4.8 copy-start.6
  269.2 0.9 copy-start.2
  278.9 0.9 copy-start.10
  283.6 7.3 %copy-start.9 = (f32[768]{0:T(1024)S(1)}, f32[768]{0:T(1024)}, u32[]{:S(2)}) copy-start(f32[768]{0:T(1024)} %param.21) | copy-start | bytes 9220
  289.5 0.8 copy-start.3
Sparse Core Ops, SparseCore 0:
  112.8 127.1 all-gather.1
  300.2 238.7 all-reduce.1
